TPU v7x, 32 devices: a whole 2x2x4 slice. The times are simulated.
32 devices in a mesh: rows: 8 (over y, x, core), gz: 4 (over z).
Axes of the slice: x: 2, y: 2, z: 4, core: 2. Of those that a mesh axis runs over, the one named last changes fastest.
Arguments:
- plane_colour_samples: int32 [8, 3, 256, 2048], P('gz', None, 'rows'), may hold values from 0 to 255
- clarity_gain: float32 [8], P('gz'), may hold values from 0.01 to 4
Outputs:
- joined: float32 [3, 256, 2048], P(None, 'rows')
All inputs are finite; a program needn't handle non-finite values.
Results may differ from a plain program's by a relative error of at most 0.000067.
Values sent between devices are 32-bit elements; how exact they have to be, the bound alone decides.
A program may use at most 64 MiB of HBM per device.

v0:
```python
import functools

import jax
import jax.numpy as jnp
import ml_dtypes
import numpy as np
from jax import lax
from jax.experimental import pallas as pl
from jax.experimental.pallas import tpu as pltpu
from jax.sharding import PartitionSpec as P

MESH = pl.DeviceIdType.MESH
F32 = jnp.float32
BF16 = jnp.bfloat16
TAPS = (1 / 16, 4 / 16, 6 / 16, 4 / 16, 1 / 16)


def down_rows(rows_in):
    m = np.zeros((rows_in // 2, rows_in), np.float32)
    for i in range(rows_in // 2):
        for t, tap in enumerate(TAPS):
            if 0 <= 2 * i + t - 2 < rows_in:
                m[i, 2 * i + t - 2] = tap
    return m


def up_rows(rows_in, rows_out, first):
    m = np.zeros((rows_out, rows_in), np.float32)
    for i in range(rows_out):
        k = first + i // 2
        pairs = ((k - 1, 1 / 8), (k, 6 / 8), (k + 1, 1 / 8)) if i % 2 == 0 else ((k, 1 / 2), (k + 1, 1 / 2))
        for r, tap in pairs:
            if 0 <= r < rows_in:
                m[i, r] = tap
    return m


def down_block():
    m = np.zeros((768, 256), np.float32)
    for o in range(256):
        for t, tap in enumerate(TAPS):
            m[128 + 2 * o + t - 2, o] = tap
    return m


def up_block():
    m = np.zeros((512, 512), np.float32)
    for k in range(256):
        m[127 + k, 2 * k] = m[129 + k, 2 * k] = 1 / 8
        m[128 + k, 2 * k] = 6 / 8
        m[128 + k, 2 * k + 1] = m[129 + k, 2 * k + 1] = 1 / 2
    return m


def twice(count, matrix):
    diagonal = np.kron(np.eye(count, dtype=np.float32), matrix)
    return np.concatenate([diagonal, diagonal], axis=1)


def dot(a, b):
    return lax.dot_general(a, b, (((1,), (0,)), ((), ())), preferred_element_type=F32)


def terms(v):
    high = v.astype(BF16)
    return high, (v - high.astype(F32)).astype(BF16)


def folded(v, stacked):
    if not stacked:
        return v
    rows = v.shape[0] // 2
    return v[:rows] + v[rows:]


def col_down(source, matrix, width, put, stacked=True):
    for j in range(width // 512):
        first = 512 * j - 128
        low, high = max(0, first), min(width, first + 768)
        taps = matrix[low - first : high - first, :]
        put(256 * j, 256, folded(dot(source(low, high), taps), stacked))


def col_up(source, matrix, width, put):
    for j in range(width // 256):
        first = 256 * j - 128
        low, high = max(0, first), min(width, first + 512)
        taps = matrix[low - first : high - first, :]
        put(512 * j, 512, folded(dot(source(low, high), taps), True))


def row_apply(matrix, read, width, put):
    for low in range(0, width, 512):
        put(low, 512, dot(matrix, jnp.concatenate(terms(read(low, low + 512)), axis=0)))


def kernel(
    n_rows, n_gz, planes, colours, strip, width,
    x_hbm, gain_ref, *refs,
):
    constants, out_ref, rest = refs[:9], refs[9], refs[10:]
    copied, rest = rest[:9], rest[9:]
    body(n_rows, n_gz, planes, colours, strip, width, x_hbm, gain_ref, constants, copied, out_ref, *rest)


def body(
    n_rows, n_gz, planes, colours, strip, width, x_hbm, gain_ref, constants, copied, out_ref,
    x_ref, x_sem, const_sem,
    grey, sq, xb, cext, l1, l2, st, up2, detail, logit, lse, lse_in, lse_fin, w0, cw, cw2, w1, w2, c1, part, part_in,
    h_send, h_recv, e_send, e_recv, eo_send, eo_recv, j_send, j_recv, jo_send, jo_recv,
):
    pc = planes * colours
    half, quarter = strip // 2, strip // 4
    ext0, ext1, ext2 = strip + 32, half + 16, quarter + 8
    w_half, w_quarter = width // 2, width // 4
    r = lax.axis_index("rows")
    z = lax.axis_index("gz")
    has_up, has_down = r > 0, r < n_rows - 1
    upper, lower = jnp.maximum(r - 1, 0), jnp.minimum(r + 1, n_rows - 1)
    left = z < n_gz // 2
    inward = jnp.where(left, z + 1, z - 1)
    has_outer = jnp.logical_and(z > 0, z < n_gz - 1)
    outward = jnp.where(has_outer, jnp.where(left, z - 1, z + 1), z)
    is_mid = jnp.logical_or(z == n_gz // 2 - 1, z == n_gz // 2)
    slot = jnp.where(is_mid, 1, 0)
    not_mid = jnp.logical_not(is_mid)

    dcol_ref, ucol_ref, d1x_ref, d1w_ref, d2x_ref, d2w_ref, u2x_ref, u2b_ref, u1_ref = copied
    loads = [pltpu.make_async_copy(x_hbm.at[p], x_ref.at[p], x_sem.at[p]) for p in range(planes)]
    fetches = [pltpu.make_async_copy(a, b, const_sem.at[k]) for k, (a, b) in enumerate(zip(constants, copied))]
    for copy in loads + fetches:
        copy.start()

    barrier = pltpu.get_barrier_semaphore()

    def greet(cond, device):
        @pl.when(cond)
        def _():
            pl.semaphore_signal(barrier, inc=1, device_id=device, device_id_type=MESH)

    greet(has_up, {"rows": upper})
    greet(has_down, {"rows": lower})
    greet(has_outer, {"gz": outward})
    pl.semaphore_signal(barrier, inc=1, device_id={"gz": inward}, device_id_type=MESH)

    for p in range(planes):
        loads[p].wait()
        samples = [x_ref[p, c].astype(F32) for c in range(colours)]
        for c in range(colours):
            xb[pl.ds((p * colours + c) * strip, strip), :] = samples[c].astype(BF16)
        mixed = 0.299 * samples[0] + 0.587 * samples[1] + 0.114 * samples[2]
        grey[p, pl.ds(8, strip), :width] = mixed * (1.0 / 255.0)
        grey[p, pl.ds(8, strip), width:] = jnp.zeros((strip, 128), F32)

    @pl.when(jnp.logical_not(has_up))
    def _():
        grey[:, 0:8, :] = jnp.zeros((planes, 8, width + 128), F32)
        cext[:, :, 0:16, :] = jnp.zeros((planes, colours, 16, w_half), F32)
        cw[:, 0:16, :] = jnp.zeros((planes, 16, w_half), F32)

    @pl.when(jnp.logical_not(has_down))
    def _():
        grey[:, strip + 8 :, :] = jnp.zeros((planes, 8, width + 128), F32)
        cext[:, :, strip + 16 :, :] = jnp.zeros((planes, colours, 16, w_half), F32)
        cw[:, strip + 16 :, :] = jnp.zeros((planes, 16, w_half), F32)

    pl.semaphore_wait(
        barrier, 1 + has_up.astype(jnp.int32) + has_down.astype(jnp.int32) + has_outer.astype(jnp.int32)
    )

    def halo(kind, ref, lead, depth):
        def view(first):
            return ref.at[(slice(None),) * lead + (pl.ds(first, depth), slice(None))]

        def copies():
            up = pltpu.make_async_remote_copy(
                src_ref=view(depth), dst_ref=view(strip + depth),
                send_sem=h_send.at[kind, 0], recv_sem=h_recv.at[kind, 0],
                device_id={"rows": upper}, device_id_type=MESH,
            )
            down = pltpu.make_async_remote_copy(
                src_ref=view(strip), dst_ref=view(0),
                send_sem=h_send.at[kind, 1], recv_sem=h_recv.at[kind, 1],
                device_id={"rows": lower}, device_id_type=MESH,
            )
            return up, down

        def start():
            up, down = copies()
            pl.when(has_up)(up.start)
            pl.when(has_down)(down.start)

        def arrived():
            up, down = copies()
            pl.when(has_down)(up.wait_recv)
            pl.when(has_up)(down.wait_recv)

        def sent():
            up, down = copies()
            pl.when(has_up)(up.wait_send)
            pl.when(has_down)(down.wait_send)

        return start, arrived, sent

    def chain(own, arrive, final, send, recv, out_send, out_recv):
        def inner(view, k, s):
            return pltpu.make_async_remote_copy(
                src_ref=own.at[view], dst_ref=arrive.at[(s,) + view],
                send_sem=send.at[k], recv_sem=recv.at[s, k],
                device_id={"gz": inward}, device_id_type=MESH,
            )

        def outer(view, k):
            return pltpu.make_async_remote_copy(
                src_ref=final.at[view], dst_ref=final.at[view],
                send_sem=out_send.at[k], recv_sem=out_recv.at[k],
                device_id={"gz": outward}, device_id_type=MESH,
            )

        return inner, outer

    grey_start, grey_arrived, grey_sent = halo(0, grey, 1, 8)
    image_start, image_arrived, image_sent = halo(1, cext, 2, 16)
    weight_start, weight_arrived, weight_sent = halo(2, cw, 1, 16)
    e_inner, e_outer = chain(lse, lse_in, lse_fin, e_send, e_recv, eo_send, eo_recv)
    j_inner, j_outer = chain(part, part_in, out_ref, j_send, j_recv, jo_send, jo_recv)

    grey_start()
    for copy in fetches:
        copy.wait()

    def put_c(low, count, v):
        cext[:, :, pl.ds(16, strip), low : low + count] = (v * (1.0 / 255.0)).reshape(planes, colours, strip, count)

    col_down(lambda a, b: xb[:, a:b], dcol_ref, width, put_c, False)
    image_start()

    padded = width + 128
    e_chunks = [(pl.ds(8 * t, 8), slice(None)) for t in range(strip // 8)]

    def square(p, i):
        line = lax.broadcasted_iota(jnp.int32, (8, padded), 0) + (r * strip - 4 + 8 * i)
        column = lax.broadcasted_iota(jnp.int32, (8, padded), 1)
        inside = (line >= 0) & (line < strip * n_rows) & (column < width)
        centre = grey[p, pl.ds(4 + 8 * i, 8), :]
        lap = 4.0 * centre - grey[p, pl.ds(3 + 8 * i, 8), :] - grey[p, pl.ds(5 + 8 * i, 8), :]
        lap = lap - pltpu.roll(centre, 1, 1) - pltpu.roll(centre, padded - 1, 1)
        lap = jnp.where(inside, lap, 0.0)
        sq[p, pl.ds(8 * i, 8), :] = lap * lap

    def merge(a, b):
        return jnp.maximum(a, b) + jnp.log(1.0 + jnp.exp(-jnp.abs(a - b)))

    def clarity(t):
        rows = pl.ds(8 * t, 8)
        top = None
        for p in range(planes):
            total = sq[p, rows, :]
            for k in range(1, 9):
                total = total + sq[p, pl.ds(8 * t + k, 8), :]
            two = total + pltpu.roll(total, 1, 1)
            four = two + pltpu.roll(two, 2, 1)
            eight = four + pltpu.roll(four, 4, 1)
            nine = eight + pltpu.roll(total, 8, 1)
            energy = pltpu.roll(nine, padded - 4, 1)
            scaled = energy[:, :width] * gain_ref[p]
            logit[p, rows, :] = scaled
            top = scaled if top is None else merge(top, scaled)
        lse[rows, :] = top

        @pl.when(jnp.logical_not(has_outer))
        def _():
            e_inner(e_chunks[t], t, slot).start()

    last = strip // 8
    for i in range(1, last):
        for p in range(planes):
            square(p, i)
    for t in range(1, last - 1):
        clarity(t)

    grey_arrived()
    for p in range(planes):
        square(p, 0)
        square(p, last)
    e_order = list(range(1, last - 1)) + sorted({0, last - 1})
    for t in e_order[last - 2 :]:
        clarity(t)

    @pl.when(has_outer)
    def _():
        for k in e_order:
            view = e_chunks[k]
            e_inner(view, k, 0).wait_recv()
            lse[view] = merge(lse[view], lse_in[(0,) + view])
            e_inner(view, k, slot).start()

    @pl.when(is_mid)
    def _():
        for k in e_order:
            view = e_chunks[k]
            e_inner(view, k, 1).wait_recv()
            lse_fin[view] = merge(lse[view], lse_in[(1,) + view])
            pl.when(has_outer)(e_outer(view, k).start)

    image_arrived()

    def edge_mask(rows_ext, margin, rows_own):
        row = lax.broadcasted_iota(jnp.int32, (rows_ext, 512), 0) + (r * rows_own - margin)
        return ((row >= 0) & (row < rows_own * n_rows)).astype(F32)[None]

    mask1 = edge_mask(ext1, 8, half)
    mask2 = edge_mask(ext2, 4, quarter)
    for p in range(planes):
        def put_l1(low, count, v):
            l1[p, :, :, low : low + count] = v.reshape(colours, ext1, count) * mask1

        row_apply(d1x_ref[...], lambda a, b: cext[p, :, :, a:b].reshape(colours * ext0, b - a), w_half, put_l1)

    def stage(rows, low, count, v, base=0):
        size = v.shape[0]
        high, rest = terms(v)
        st[pl.ds(base, size), low : low + count] = high
        st[pl.ds(rows + base, size), low : low + count] = rest

    def staged(rows):
        return lambda a, b: st[0 : 2 * rows, a:b]

    full = colours * strip
    for p in range(planes):
        row_apply(
            u1_ref[...], lambda a, b: l1[p, :, :, a:b].reshape(colours * ext1, b - a), w_half,
            functools.partial(stage, planes * full, base=p * full),
        )

    def put_detail(low, count, v):
        samples = xb[:, low : low + count].astype(F32)
        detail[:, :, :, low : low + count] = (samples * (1.0 / 255.0) - v).reshape(planes, colours, strip, count)

    col_up(staged(planes * full), ucol_ref, w_half, put_detail)

    @pl.when(not_mid)
    def _():
        for k in e_order:
            e_outer(e_chunks[k], k).wait_recv()
            pl.when(has_outer)(e_outer(e_chunks[k], k).start)

    for t in range(strip // 8):
        view = e_chunks[t]
        for p in range(planes):
            w0[(p,) + view] = jnp.exp(logit[(p,) + view] - lse_fin[view])

    own_rows = planes * strip
    for low in range(0, width, 512):
        stage(own_rows, low, 512, w0[:, :, low : low + 512].reshape(own_rows, 512))

    def put_cw(low, count, v):
        cw[:, pl.ds(16, strip), low : low + count] = v.reshape(planes, strip, count)

    col_down(staged(own_rows), dcol_ref, width, put_cw)
    weight_start()

    for low in range(0, width, 512):
        for c in range(colours):
            acc = w0[0, :, low : low + 512] * detail[0, c, :, low : low + 512]
            for p in range(1, planes):
                acc = acc + w0[p, :, low : low + 512] * detail[p, c, :, low : low + 512]
            part[c, :, low : low + 512] = acc

    rows1 = pc * ext1
    for low in range(0, w_half, 512):
        stage(rows1, low, 512, l1[:, :, :, low : low + 512].reshape(rows1, 512))

    def put_c2(low, count, v):
        up2[:, low : low + count] = v

    col_down(staged(rows1), dcol_ref, w_half, put_c2)

    def put_l2(low, count, v):
        l2[:, :, :, low : low + count] = (v.reshape(pc, ext2, count) * mask2).reshape(planes, colours, ext2, count)

    row_apply(d2x_ref[...], lambda a, b: up2[:, a:b], w_quarter, put_l2)
    row_apply(
        u2x_ref[...], lambda a, b: l2[:, :, :, a:b].reshape(pc * ext2, b - a), w_quarter,
        functools.partial(stage, rows1),
    )

    def put_up2(low, count, v):
        up2[:, low : low + count] = v

    col_up(staged(rows1), ucol_ref, w_quarter, put_up2)

    weight_arrived()
    w_rows = planes * ext0

    def put_w1(low, count, v):
        w1[:, :, low : low + count] = v.reshape(planes, ext1, count) * mask1

    row_apply(d1w_ref[...], lambda a, b: cw[:, :, a:b].reshape(w_rows, b - a), w_half, put_w1)
    w1_rows = planes * ext1
    for low in range(0, w_half, 512):
        stage(w1_rows, low, 512, w1[:, :, low : low + 512].reshape(w1_rows, 512))

    def put_cw2(low, count, v):
        cw2[:, low : low + count] = v

    col_down(staged(w1_rows), dcol_ref, w_half, put_cw2)

    def put_w2(low, count, v):
        w2[:, :, low : low + count] = v.reshape(planes, ext2, count) * mask2

    row_apply(d2w_ref[...], lambda a, b: cw2[:, a:b], w_quarter, put_w2)

    def read_b2(a, b):
        acc = w2[0, :, a:b][None] * l2[0, :, :, a:b]
        for p in range(1, planes):
            acc = acc + w2[p, :, a:b][None] * l2[p, :, :, a:b]
        return acc.reshape(colours * ext2, b - a)

    rows_c1 = colours * ext1
    row_apply(u2b_ref[...], read_b2, w_quarter, functools.partial(stage, rows_c1))

    def put_c1(low, count, v):
        acc = v.reshape(colours, ext1, count)
        for p in range(planes):
            first = p * rows_c1
            coarse = up2[pl.ds(first, rows_c1), low : low + count].reshape(colours, ext1, count)
            acc = acc + w1[p, :, low : low + count][None] * (l1[p, :, :, low : low + count] - coarse)
        c1[:, :, low : low + count] = acc * mask1

    col_up(staged(rows_c1), ucol_ref, w_quarter, put_c1)

    row_apply(
        u1_ref[...], lambda a, b: c1[:, :, a:b].reshape(rows_c1, b - a), w_half, functools.partial(stage, full)
    )

    j_chunks = [(c, slice(None), slice(low, low + 512)) for low in range(0, width, 512) for c in range(colours)]

    def into(k):
        view = j_chunks[k]

        @pl.when(has_outer)
        def _():
            j_inner(view, k, 0).wait_recv()
            part[view] = part[view] + part_in[(0,) + view]
            j_inner(view, k, slot).start()

    lag = 3

    def step(k):
        if k < len(j_chunks):
            into(k)
        if k >= lag:
            view = j_chunks[k - lag]

            @pl.when(is_mid)
            def _():
                j_inner(view, k - lag, 1).wait_recv()
                out_ref[view] = part[view] + part_in[(1,) + view]
                pl.when(has_outer)(j_outer(view, k - lag).start)

    def put_part(low, count, v):
        part[:, :, low : low + count] += v.reshape(colours, strip, count)

        @pl.when(jnp.logical_not(has_outer))
        def _():
            for c in range(colours):
                k = low // count * colours + c
                j_inner(j_chunks[k], k, slot).start()

        for k in range(max(0, low // count - 1) * colours, low // count * colours):
            step(k)

    col_up(staged(full), ucol_ref, w_half, put_part)

    for k in range(len(j_chunks) - colours, len(j_chunks) + lag):
        step(k)

    @pl.when(not_mid)
    def _():
        for k, view in enumerate(j_chunks):
            j_outer(view, k).wait_recv()
            pl.when(has_outer)(j_outer(view, k).start)

    grey_sent()
    image_sent()
    weight_sent()
    for k, view in enumerate(e_chunks):
        e_inner(view, k, slot).wait_send()
        pl.when(has_outer)(e_outer(view, k).wait_send)
    for k, view in enumerate(j_chunks):
        j_inner(view, k, slot).wait_send()
        pl.when(has_outer)(j_outer(view, k).wait_send)


def on_device(n_rows, n_gz, samples, gain):
    planes, colours, strip, width = samples.shape
    pc = planes * colours
    half, quarter = strip // 2, strip // 4
    ext0, ext1, ext2 = strip + 32, half + 16, quarter + 8
    d1, d2 = down_rows(ext0), down_rows(ext1)
    u2, u1 = up_rows(ext2, ext1, 0), up_rows(ext1, strip, 8)
    constants = [
        down_block(), up_block(), twice(colours, d1), twice(planes, d1), twice(pc, d2), twice(planes, d2),
        twice(pc, u2), twice(colours, u2), twice(colours, u1),
    ]
    constants = [jnp.asarray(c.astype(ml_dtypes.bfloat16)) for c in constants]
    n_e, n_j = strip // 8, colours * width // 512
    dma = pltpu.SemaphoreType.DMA
    vmem = pl.BlockSpec(memory_space=pltpu.VMEM)
    hbm = pl.BlockSpec(memory_space=pltpu.HBM)
    return pl.pallas_call(
        functools.partial(kernel, n_rows, n_gz, planes, colours, strip, width),
        out_shape=jax.ShapeDtypeStruct((colours, strip, width), F32),
        in_specs=[hbm, pl.BlockSpec(memory_space=pltpu.SMEM)] + [hbm] * len(constants),
        out_specs=vmem,
        scratch_shapes=[pltpu.VMEM(c.shape, c.dtype) for c in constants] + [
            pltpu.VMEM(samples.shape, samples.dtype),
            dma((planes,)), dma((len(constants),)),
            pltpu.VMEM((planes, strip + 16, width + 128), F32),
            pltpu.VMEM((planes, strip + 8, width + 128), F32),
            pltpu.VMEM((pc * strip, width), BF16),
            pltpu.VMEM((planes, colours, ext0, width // 2), F32),
            pltpu.VMEM((planes, colours, ext1, width // 2), F32),
            pltpu.VMEM((planes, colours, ext2, width // 4), F32),
            pltpu.VMEM((2 * max(pc * ext1, pc * strip), width), BF16),
            pltpu.VMEM((pc * ext1, width // 2), F32),
            pltpu.VMEM((planes, colours, strip, width), F32),
            pltpu.VMEM((planes, strip, width), F32),
            pltpu.VMEM((strip, width), F32),
            pltpu.VMEM((2, strip, width), F32),
            pltpu.VMEM((strip, width), F32),
            pltpu.VMEM((planes, strip, width), F32),
            pltpu.VMEM((planes, ext0, width // 2), F32),
            pltpu.VMEM((planes * ext1, width // 4), F32),
            pltpu.VMEM((planes, ext1, width // 2), F32),
            pltpu.VMEM((planes, ext2, width // 4), F32),
            pltpu.VMEM((colours, ext1, width // 2), F32),
            pltpu.VMEM((colours, strip, width), F32),
            pltpu.VMEM((2, colours, strip, width), F32),
            dma((3, 2)), dma((3, 2)),
            dma((n_e,)), dma((2, n_e)), dma((n_e,)), dma((n_e,)),
            dma((n_j,)), dma((2, n_j)), dma((n_j,)), dma((n_j,)),
        ],
        compiler_params=pltpu.CompilerParams(
            collective_id=0, has_side_effects=True, vmem_limit_bytes=56 * 1024 * 1024
        ),
    )(samples, gain, *constants)


def solution(mesh):
    return jax.shard_map(
        functools.partial(on_device, mesh.shape["rows"], mesh.shape["gz"]),
        mesh=mesh,
        in_specs=(P("gz", None, "rows", None), P("gz")),
        out_specs=P(None, "rows", None),
        check_vma=False,
    )
```

profile of v0, /device:TPU:3, one launch (start us, length us, event | category | flops | bytes accessed | tf_op | source)
XLA Modules:
  0.0 56.5 jit_solution(282399164876373270)
XLA Ops:
  0.0 54.5 %shard_map.109 = f32[3,32,2048]{2,1,0:T(8,128)} custom-call(s32[2,3,32,2048]{3,2,1,0:T(8,128)} %x_hbm.1, f32[2]{0:T(128)} %gain_ref.1, bf16[768,256]{1,0:T(8,128)(2,1)} %constant.18.clone.refs_0_, bf16[512,512]{1,0:T(8,128)(2,1)} %constant.19.clone.refs_1_, bf16[96,384]{1,0:T(8,128)(2,1)} %constant.20.clone.refs_2_, bf16[64,256]{1,0:T(8,128)(2,1)} %constant.21.clone.refs_3_, ...), custom_call_target="tpu_custom_call" | custom-call | tf_op jit(solution)/shard_map/pallas_call | solution.py:512
  54.5 2.1 %copy.13 = f32[3,32,2048]{2,1,0:T(8,128)} copy(f32[3,32,2048]{2,1,0:T(8,128)} %shard_map.109) | data formatting | bytes 1572864
where the time goes:
time: 56.8 us; the launch traced here: 56.5 us
  Pallas kernels  54.5 us (96%)
  local copies, waits for them, and re-layouts  2.06 us (4%)
    pallas_call x1, Pallas kernels, on_device(): pl.pallas_call(functools.partial(kernel, n_rows, n_gz, planes, colours, s...  54.5 us
    unnamed x1, local copies, waits for them, and re-layouts  2.06 us

commit v1 on v0

--- a/solution.py
+++ b/solution.py
@@ -108,7 +108,9 @@
     x_ref, x_sem, const_sem,
     grey, sq, xb, cext, l1, l2, st, up2, detail, logit, lse, lse_in, lse_fin, w0, cw, cw2, w1, w2, c1, part, part_in,
     h_send, h_recv, e_send, e_recv, eo_send, eo_recv, j_send, j_recv, jo_send, jo_recv,
+    final, final_sem, *halos,
 ):
+    image_halos, weight_halos = halos[:4], halos[4:]
     pc = planes * colours
     half, quarter = strip // 2, strip // 4
     ext0, ext1, ext2 = strip + 32, half + 16, quarter + 8
@@ -155,14 +157,14 @@
     @pl.when(jnp.logical_not(has_up))
     def _():
         grey[:, 0:8, :] = jnp.zeros((planes, 8, width + 128), F32)
-        cext[:, :, 0:16, :] = jnp.zeros((planes, colours, 16, w_half), F32)
-        cw[:, 0:16, :] = jnp.zeros((planes, 16, w_half), F32)
 
     @pl.when(jnp.logical_not(has_down))
     def _():
         grey[:, strip + 8 :, :] = jnp.zeros((planes, 8, width + 128), F32)
-        cext[:, :, strip + 16 :, :] = jnp.zeros((planes, colours, 16, w_half), F32)
-        cw[:, strip + 16 :, :] = jnp.zeros((planes, 16, w_half), F32)
+
+    for low in (0, strip + 16):
+        cext[:, :, pl.ds(low, 16), :] = jnp.zeros((planes, colours, 16, w_half), F32)
+        cw[:, pl.ds(low, 16), :] = jnp.zeros((planes, 16, w_half), F32)
 
     pl.semaphore_wait(
         barrier, 1 + has_up.astype(jnp.int32) + has_down.astype(jnp.int32) + has_outer.astype(jnp.int32)
@@ -202,6 +204,55 @@
 
         return start, arrived, sent
 
+    def packed_halo(kind, arrays, to_up, to_down, from_up, from_down):
+        def copies():
+            up = pltpu.make_async_remote_copy(
+                src_ref=to_up, dst_ref=from_down, send_sem=h_send.at[kind, 0], recv_sem=h_recv.at[kind, 0],
+                device_id={"rows": upper}, device_id_type=MESH,
+            )
+            down = pltpu.make_async_remote_copy(
+                src_ref=to_down, dst_ref=from_up, send_sem=h_send.at[kind, 1], recv_sem=h_recv.at[kind, 1],
+                device_id={"rows": lower}, device_id_type=MESH,
+            )
+            return up, down
+
+        def start():
+            up, down = copies()
+
+            @pl.when(has_up)
+            def _():
+                for i, (ref, lead) in enumerate(arrays):
+                    to_up[pl.ds(11 * i, 11), :] = ref[lead + (pl.ds(16, 11), slice(None))]
+                up.start()
+
+            @pl.when(has_down)
+            def _():
+                for i, (ref, lead) in enumerate(arrays):
+                    to_down[pl.ds(10 * i, 10), :] = ref[lead + (pl.ds(strip + 6, 10), slice(None))]
+                down.start()
+
+        def arrived():
+            up, down = copies()
+
+            @pl.when(has_down)
+            def _():
+                up.wait_recv()
+                for i, (ref, lead) in enumerate(arrays):
+                    ref[lead + (pl.ds(strip + 16, 11), slice(None))] = from_down[pl.ds(11 * i, 11), :]
+
+            @pl.when(has_up)
+            def _():
+                down.wait_recv()
+                for i, (ref, lead) in enumerate(arrays):
+                    ref[lead + (pl.ds(6, 10), slice(None))] = from_up[pl.ds(10 * i, 10), :]
+
+        def sent():
+            up, down = copies()
+            pl.when(has_up)(up.wait_send)
+            pl.when(has_down)(down.wait_send)
+
+        return start, arrived, sent
+
     def chain(own, arrive, final, send, recv, out_send, out_recv):
         def inner(view, k, s):
             return pltpu.make_async_remote_copy(
@@ -220,10 +271,12 @@
         return inner, outer
 
     grey_start, grey_arrived, grey_sent = halo(0, grey, 1, 8)
-    image_start, image_arrived, image_sent = halo(1, cext, 2, 16)
-    weight_start, weight_arrived, weight_sent = halo(2, cw, 1, 16)
+    image_start, image_arrived, image_sent = packed_halo(
+        1, [(cext, (p, c)) for p in range(planes) for c in range(colours)], *image_halos
+    )
+    weight_start, weight_arrived, weight_sent = packed_halo(2, [(cw, (p,)) for p in range(planes)], *weight_halos)
     e_inner, e_outer = chain(lse, lse_in, lse_fin, e_send, e_recv, eo_send, eo_recv)
-    j_inner, j_outer = chain(part, part_in, out_ref, j_send, j_recv, jo_send, jo_recv)
+    j_inner, j_outer = chain(part, part_in, final, j_send, j_recv, jo_send, jo_recv)
 
     grey_start()
     for copy in fetches:
@@ -447,6 +500,9 @@
 
     lag = 3
 
+    def store(k):
+        return pltpu.make_async_copy(final.at[j_chunks[k]], out_ref.at[j_chunks[k]], final_sem.at[k])
+
     def step(k):
         if k < len(j_chunks):
             into(k)
@@ -456,8 +512,9 @@
             @pl.when(is_mid)
             def _():
                 j_inner(view, k - lag, 1).wait_recv()
-                out_ref[view] = part[view] + part_in[(1,) + view]
+                final[view] = part[view] + part_in[(1,) + view]
                 pl.when(has_outer)(j_outer(view, k - lag).start)
+                store(k - lag).start()
 
     def put_part(low, count, v):
         part[:, :, low : low + count] += v.reshape(colours, strip, count)
@@ -481,6 +538,7 @@
         for k, view in enumerate(j_chunks):
             j_outer(view, k).wait_recv()
             pl.when(has_outer)(j_outer(view, k).start)
+            store(k).start()
 
     grey_sent()
     image_sent()
@@ -490,6 +548,7 @@
         pl.when(has_outer)(e_outer(view, k).wait_send)
     for k, view in enumerate(j_chunks):
         j_inner(view, k, slot).wait_send()
+        store(k).wait()
         pl.when(has_outer)(j_outer(view, k).wait_send)
 
 
@@ -507,13 +566,12 @@
     constants = [jnp.asarray(c.astype(ml_dtypes.bfloat16)) for c in constants]
     n_e, n_j = strip // 8, colours * width // 512
     dma = pltpu.SemaphoreType.DMA
-    vmem = pl.BlockSpec(memory_space=pltpu.VMEM)
     hbm = pl.BlockSpec(memory_space=pltpu.HBM)
     return pl.pallas_call(
         functools.partial(kernel, n_rows, n_gz, planes, colours, strip, width),
         out_shape=jax.ShapeDtypeStruct((colours, strip, width), F32),
         in_specs=[hbm, pl.BlockSpec(memory_space=pltpu.SMEM)] + [hbm] * len(constants),
-        out_specs=vmem,
+        out_specs=hbm,
         scratch_shapes=[pltpu.VMEM(c.shape, c.dtype) for c in constants] + [
             pltpu.VMEM(samples.shape, samples.dtype),
             dma((planes,)), dma((len(constants),)),
@@ -541,6 +599,10 @@
             dma((3, 2)), dma((3, 2)),
             dma((n_e,)), dma((2, n_e)), dma((n_e,)), dma((n_e,)),
             dma((n_j,)), dma((2, n_j)), dma((n_j,)), dma((n_j,)),
+            pltpu.VMEM((colours, strip, width), F32), dma((n_j,)),
+        ] + [
+            pltpu.VMEM((-(-count * rows // 8) * 8, width // 2), F32)
+            for count in (pc, planes) for rows in (11, 10, 10, 11)
         ],
         compiler_params=pltpu.CompilerParams(
             collective_id=0, has_side_effects=True, vmem_limit_bytes=56 * 1024 * 1024

time: 56.8 us -> 56.3 us (level)
  no operation moved by 1% of the time
where the time goes in v1:
time: 56.3 us; the launch traced here: 56.1 us
  Pallas kernels  54 us (96%)
  local copies, waits for them, and re-layouts  2.06 us (4%)
    pallas_call x1, Pallas kernels, on_device(): pl.pallas_call(functools.partial(kernel, n_rows, n_gz, planes, colours, s...  54 us
    unnamed x1, local copies, waits for them, and re-layouts  2.06 us

profile of v1, /device:TPU:3, one launch (start us, length us, event | category | flops | bytes accessed | tf_op | source)
XLA Modules:
  0.0 56.1 jit_solution(16924164922110927634)
XLA Ops:
  0.0 54.0 %shard_map.109 = f32[3,32,2048]{2,1,0:T(8,128)} custom-call(s32[2,3,32,2048]{3,2,1,0:T(8,128)} %x_hbm.1, f32[2]{0:T(128)} %gain_ref.1, bf16[768,256]{1,0:T(8,128)(2,1)} %constant.18.clone.refs_0_, bf16[512,512]{1,0:T(8,128)(2,1)} %constant.19.clone.refs_1_, bf16[96,384]{1,0:T(8,128)(2,1)} %constant.20.clone.refs_2_, bf16[64,256]{1,0:T(8,128)(2,1)} %constant.21.clone.refs_3_, ...), custom_call_target="tpu_custom_call" | custom-call | tf_op jit(solution)/shard_map/pallas_call | solution.py:570
  54.0 2.1 %copy.13 = f32[3,32,2048]{2,1,0:T(8,128)} copy(f32[3,32,2048]{2,1,0:T(8,128)} %shard_map.109) | data formatting | bytes 1572864

commit v2 on v1

--- a/solution.py
+++ b/solution.py
@@ -279,15 +279,6 @@
     j_inner, j_outer = chain(part, part_in, final, j_send, j_recv, jo_send, jo_recv)
 
     grey_start()
-    for copy in fetches:
-        copy.wait()
-
-    def put_c(low, count, v):
-        cext[:, :, pl.ds(16, strip), low : low + count] = (v * (1.0 / 255.0)).reshape(planes, colours, strip, count)
-
-    col_down(lambda a, b: xb[:, a:b], dcol_ref, width, put_c, False)
-    image_start()
-
     padded = width + 128
     e_chunks = [(pl.ds(8 * t, 8), slice(None)) for t in range(strip // 8)]
 
@@ -332,21 +323,35 @@
     for t in range(1, last - 1):
         clarity(t)
 
+    for copy in fetches:
+        copy.wait()
+
+    def put_c(low, count, v):
+        cext[:, :, pl.ds(16, strip), low : low + count] = (v * (1.0 / 255.0)).reshape(planes, colours, strip, count)
+
+    col_down(lambda a, b: xb[:, a:b], dcol_ref, width, put_c, False)
+    image_start()
+
+    e_order = list(range(1, last - 1)) + sorted({0, last - 1})
+
+    def forward(chunks):
+        @pl.when(has_outer)
+        def _():
+            for k in chunks:
+                view = e_chunks[k]
+                e_inner(view, k, 0).wait_recv()
+                lse[view] = merge(lse[view], lse_in[(0,) + view])
+                e_inner(view, k, slot).start()
+
+    forward(e_order[: last - 2])
     grey_arrived()
     for p in range(planes):
         square(p, 0)
         square(p, last)
-    e_order = list(range(1, last - 1)) + sorted({0, last - 1})
     for t in e_order[last - 2 :]:
         clarity(t)
 
-    @pl.when(has_outer)
-    def _():
-        for k in e_order:
-            view = e_chunks[k]
-            e_inner(view, k, 0).wait_recv()
-            lse[view] = merge(lse[view], lse_in[(0,) + view])
-            e_inner(view, k, slot).start()
+    forward(e_order[last - 2 :])
 
     @pl.when(is_mid)
     def _():

time: 56.3 us -> 55.7 us (0.989)
  Pallas kernels: 54 us -> 53 us
    pallas_call x1, Pallas kernels: 54 us -> 53 us  [on_device(): pl.pallas_call(functools.partial(kernel, n_rows, n_gz, planes, colours, s...]
where the time goes in v2:
time: 55.7 us; the launch traced here: 55.1 us
  Pallas kernels  53 us (95%)
  local copies, waits for them, and re-layouts  2.06 us (4%)
    pallas_call x1, Pallas kernels, on_device(): pl.pallas_call(functools.partial(kernel, n_rows, n_gz, planes, colours, s...  53 us
    unnamed x1, local copies, waits for them, and re-layouts  2.06 us

profile of v2, /device:TPU:3, one launch (start us, length us, event | category | flops | bytes accessed | tf_op | source)
XLA Modules:
  0.0 55.1 jit_solution(10328768716748084596)
XLA Ops:
  0.0 53.0 %shard_map.109 = f32[3,32,2048]{2,1,0:T(8,128)} custom-call(s32[2,3,32,2048]{3,2,1,0:T(8,128)} %x_hbm.1, f32[2]{0:T(128)} %gain_ref.1, bf16[768,256]{1,0:T(8,128)(2,1)} %constant.18.clone.refs_0_, bf16[512,512]{1,0:T(8,128)(2,1)} %constant.19.clone.refs_1_, bf16[96,384]{1,0:T(8,128)(2,1)} %constant.20.clone.refs_2_, bf16[64,256]{1,0:T(8,128)(2,1)} %constant.21.clone.refs_3_, ...), custom_call_target="tpu_custom_call" | custom-call | tf_op jit(solution)/shard_map/pallas_call | solution.py:575
  53.0 2.1 %copy.13 = f32[3,32,2048]{2,1,0:T(8,128)} copy(f32[3,32,2048]{2,1,0:T(8,128)} %shard_map.109) | data formatting | bytes 1572864
